TPU v7x, 256 devices: a whole 4x4x8 slice. The times are simulated.
256 devices in a mesh: pa: 16 (over z_hi, y, core), pb: 16 (over z_lo, x).
Axes of the slice: x: 4, y: 4, z: 8 (z_hi: 2, z_lo: 4; z = z_hi * 4 + z_lo), core: 2. Of those that a mesh axis runs over, the one named last changes fastest.
Arguments:
- excitons: bfloat16 [2, 512, 1024], P(None, 'pa', 'pb'), may hold values from -6 to 6
- screened: bfloat16 [16384, 16384], P('pa', 'pb'), may hold values from -0.25 to 0.25
- phi_val: bfloat16 [16384, 512], P('pa'), may hold values from -0.25 to 0.25
- phi_con: bfloat16 [16384, 1024], P('pb'), may hold values from -0.1875 to 0.1875
Outputs:
- kernel_out: bfloat16 [2, 512, 1024], P(None, 'pa', 'pb')
All inputs are finite; a program needn't handle non-finite values.
Results may differ from a plain program's by a relative error of at most 0.0057.
Values may be sent and summed in bfloat16 or wider, within the bound.
A program may use at most 64 MiB of HBM per device.

v0:
```python
import jax
import jax.numpy as jnp
from jax import lax
from jax.sharding import PartitionSpec as P


def local(excitons, screened, phi_val, phi_con):
    high = lax.Precision.HIGHEST
    val_rows = lax.all_gather(excitons, "pb", axis=2, tiled=True)
    half_exp = jnp.einsum(
        "evc,qc->evq",
        lax.all_gather(val_rows, "pa", axis=1, tiled=True),
        phi_con,
        preferred_element_type=jnp.float32,
    ).astype(jnp.bfloat16)
    expanded = jnp.einsum("pv,evq->epq", phi_val, half_exp, preferred_element_type=jnp.float32)
    weighted = (screened.astype(jnp.float32)[None] * expanded).astype(jnp.bfloat16)
    partial_value = jnp.einsum("pv,epq->evq", phi_val, weighted, preferred_element_type=jnp.float32)
    con_float = phi_con.astype(jnp.float32)
    back_val = lax.psum_scatter(partial_value, "pa", scatter_dimension=1, tiled=True)
    terms = jnp.einsum("evq,qc->evc", back_val, con_float, precision=high)
    result = lax.psum_scatter(terms, "pb", scatter_dimension=2, tiled=True)
    return result.astype(jnp.bfloat16)


def solution(mesh):
    placed = (P(None, "pa", "pb"), P("pa", "pb"), P("pa", None), P("pb", None))
    return jax.shard_map(
        local, mesh=mesh, in_specs=placed, out_specs=P(None, "pa", "pb"), check_vma=False
    )
```

profile of v0, /device:TPU:8, one launch (start us, length us, event | category | flops | bytes accessed | tf_op | source)
XLA Modules:
  0.0 425.0 jit_solution(6844575942554741751)
XLA Ops:
  6.5 1.0 copy.13
  7.5 46.5 %all_gather.6 = bf16[2,32,1024]{1,0,2:T(2,128)(2,1)S(1)} all-gather(bf16[2,32,64]{1,0,2:T(2,128)(2,1)S(1)} %copy.13), channel_id=1, replica_groups=mesh['pa'=16,'pb'=16] {'pb'}, dimensions={2}, use_global_device_ids=true | all-gather | bytes 139264 | tf_op jit(solution)/shard_map/all_gather | solution.py:9
  54.0 1.0 copy.14
  55.0 0.0 all-gather.2.cloned.1.call-update
  55.0 0.0 all-reduce.3.cloned.1.call-start
  55.1 4.1 copy.12
  59.2 56.4 %all-gather.2.cloned.1.call-done = bf16[2,512,1024]{2,0,1:T(2,128)(2,1)} async-done(((bf16[2,32,1024]{2,0,1:T(2,128)(2,1)}), bf16[2,512,1024]{2,0,1:T(2,128)(2,1)}) %all-gather.2.cloned.1.call-update) | async-done | bytes 2097168 | tf_op jit(solution)/shard_map/all_gather | solution.py:12
  115.7 5.3 %fusion.9 = bf16[2,512,1024]{2,1,0:T(8,128)(2,1)} fusion(bf16[1024,1024]{1,0:T(8,128)(2,1)S(1)} %copy-done, bf16[2,512,1024]{2,0,1:T(2,128)(2,1)} %all-gather.2.cloned.1.call-done), kind=kOutput, calls=%fused_computation.7 | convolution fusion | flops 2147483648 | bytes 6291456 | tf_op jit(solution)/shard_map/evc,qc->evq/dot_general | solution.py:10
  121.0 0.0 copy-done.1
  121.0 9.4 %fusion.4 = f32[2,512,1024]{1,2,0:T(8,128)} fusion(f32[1024,1024]{0,1:T(8,128)} %copy.12, bf16[2,512,1024]{2,1,0:T(8,128)(2,1)} %fusion.9, bf16[1024,512]{1,0:T(8,128)(2,1)S(1)} %copy-done.1), kind=kOutput, calls=%fused_computation.4 | convolution fusion | flops 4299161600 | bytes 11534336 | tf_op jit(solution)/shard_map/pv,epq->evq/dot_general | solution.py:18
  130.4 7.4 %copy.17 = f32[2,512,1024]{2,0,1:T(2,128)} copy(f32[2,512,1024]{1,2,0:T(8,128)} %fusion.4) | data formatting | bytes 8388608 | tf_op jit(solution)/shard_map/pv,epq->evq/transpose | solution.py:18
  137.7 0.0 all-reduce.3.cloned.1.call-update
  137.7 0.0 reduce-scatter.4.cloned.1.call-start
  137.8 0.6 copy-done.2
  138.4 0.6 dynamic-slice
  139.6 182.5 %all-reduce.3.cloned.1.call-done = f32[2,512,1024]{2,0,1:T(2,128)} async-done(((f32[2,512,1024]{2,0,1:T(2,128)}), f32[2,512,1024]{2,0,1:T(2,128)}) %all-reduce.3.cloned.1.call-update) | async-done | bytes 4194320
  322.1 1.0 constant_dynamic-slice_fusion
  323.1 1.3 fusion.7
  324.3 0.5 copy.20
  324.9 1.4 reshape.3
  326.3 0.0 reduce-scatter.4.cloned.1.call-update
  326.3 90.6 %reduce-scatter.4.cloned.1.call-done = f32[64,64]{1,0:T(8,128)} async-done(((f32[1024,64]{1,0:T(8,128)}), f32[64,64]{1,0:T(8,128)}) %reduce-scatter.4.cloned.1.call-update) | async-done | bytes 16400
  416.9 0.8 reshape.4
  417.7 0.7 copy.21
  (5 shorter events, 0.0 us)
Async XLA Ops:
  6.5 109.1 %copy-start = (bf16[1024,1024]{1,0:T(8,128)(2,1)S(1)}, bf16[1024,1024]{1,0:T(8,128)(2,1)}, u32[]{:S(2)}) copy-start(bf16[1024,1024]{1,0:T(8,128)(2,1)} %param.7) | copy-start | bytes 6291460
  6.5 109.1 %all-gather.2.cloned.1.call-start = ((), (), s32[]{:S(2)}) async-start(), calls=%async_computation.1 | async-start | bytes 2228224 | tf_op jit(solution)/shard_map/all_gather | solution.py:12
  55.0 267.1 %all-reduce.3.cloned.1.call-start = ((), (), s32[]{:S(2)}) async-start(), calls=%async_computation.3 | async-start | bytes 8388608
  59.2 61.8 %copy-start.1 = (bf16[1024,512]{1,0:T(8,128)(2,1)S(1)}, bf16[1024,512]{1,0:T(8,128)(2,1)}, u32[]{:S(2)}) copy-start(bf16[1024,512]{1,0:T(8,128)(2,1)} %param.6) | copy-start | bytes 3145732
  137.7 0.7 copy-start.2
  137.7 279.1 %reduce-scatter.4.cloned.1.call-start = ((), (), s32[]{:S(2)}) async-start(), calls=%async_computation.2 | async-start | bytes 557056
Sparse Core Ops, SparseCore 0:
  55.1 60.4 all-gather.1
  137.9 184.1 all-reduce.2
  326.4 90.4 reduce-scatter.3
where the time goes:
time: 425 us
  waiting for transfers between devices  330 us (78%)
  blocking collectives  46.5 us (11%)
  local copies, waits for them, and re-layouts  19.1 us (4%)
  matrix products  16 us (4%)
  between operations  13.8 us (3%)
    unnamed x5, waiting for transfers between devices  273 us
    all_gather x1, waiting for transfers between devices, local(): lax.all_gather(val_rows, 'pa', axis=1, tiled=True)  56.4 us
    all_gather x1, blocking collectives, local(): val_rows = lax.all_gather(excitons, 'pb', axis=2, tiled=True)  46.5 us
    dot_general x1, matrix products, local(): jnp.einsum('pv,epq->evq', phi_val, weighted, preferred_element_type=jnp.f...  9.39 us
  transfers between devices with their start and end apart: 3, of which 3 were waited for; matrix products, arithmetic and copies ran while one was open for 1% of the time, Pallas kernels for 0%

commit v1 on v0

v1 whole, which is shorter than its diff:
```python
import jax
import jax.numpy as jnp
from jax import lax
from jax.experimental import pallas as pl
from jax.experimental.pallas import tpu as pltpu
from jax.sharding import PartitionSpec as P

F32, BF16 = jnp.float32, jnp.bfloat16
QT = 512


def place():
    pa, pb = lax.axis_index("pa"), lax.axis_index("pb")
    return pb % 4, (pa // 2) % 4, (pa // 8) * 4 + pb // 4, pa % 2


def device(x, y, z, k):
    return ((z // 4) * 8 + y * 2 + k, (z % 4) * 4 + x)


def dot(a, b):
    return jnp.dot(a, b, preferred_element_type=F32)


def dot_nt(a, b):
    return lax.dot_general(a, b, (((1,), (1,)), ((), ())), preferred_element_type=F32)


def halves(a, b):
    low = jnp.concatenate([a[:, :64], b[:, :64]], axis=1)
    high = jnp.concatenate([a[:, 64:], b[:, 64:]], axis=1)
    return low, high


def kernel(
    exc_hbm, scr_hbm, val_hbm, con_hbm, out_ref,
    exc, tiles, got, con, conp, val, val_t, scr, xall, half, weighted, back,
    terms_f, terms, in_x, in_y, sum1_f, sum1, sum2_f, sum2, in2_y, in2_x, pack_f, pack, got3,
    loc_sem, sib_send, sib_recv, s1_send, s1_recv, s2_send, s2_recv, s3_send, s3_recv,
    r1_send, r1_recv, r1y_send, r1y_recv, r2_send, r2_recv, r3_send, r3_recv,
):
    x, y, z, k = place()
    zpeers = [(dz, dk) for dz in (4, 3, 5, 2, 6, 1, 7, 0) for dk in (0, 1) if (dz, dk) != (0, 0)]
    ring = (2, 1, 3)

    def at_z(dz, dk):
        return (z + dz) % 8, (k + dk) % 2

    def xdev(d):
        return device((x + d) % 4, y, z, k)

    def ydev(d):
        return device(x, (y + d) % 4, z, k)

    barrier = pltpu.get_barrier_semaphore()

    def greet(who):
        pl.semaphore_signal(barrier, inc=1, device_id=who, device_id_type=pl.DeviceIdType.MESH)

    for dz, dk in zpeers:
        tz, tk = at_z(dz, dk)
        greet(device(x, y, tz, tk))
    for d in ring:
        greet(xdev(d))
        greet(ydev(d))

    loads = [
        pltpu.make_async_copy(exc_hbm, exc, loc_sem.at[0]),
        pltpu.make_async_copy(con_hbm, con, loc_sem.at[1]),
        pltpu.make_async_copy(val_hbm, val.at[k], loc_sem.at[2]),
        pltpu.make_async_copy(scr_hbm, scr.at[k], loc_sem.at[3]),
    ]
    for load in loads:
        load.start()

    loads[0].wait()
    for e in range(2):
        tiles[e] = jnp.concatenate([exc[e, 0:16, :], exc[e, 16:32, :]], axis=1)
    got[z, k] = tiles[k]

    pl.semaphore_wait(barrier, len(zpeers) + 2 * len(ring))

    def remote(src, dst, send, recv, who):
        copy = pltpu.make_async_remote_copy(
            src_ref=src, dst_ref=dst, send_sem=send, recv_sem=recv, device_id=who,
            device_id_type=pl.DeviceIdType.MESH,
        )
        copy.start()
        return copy

    sent = []
    stage1 = []
    for n, (dz, dk) in enumerate(zpeers):
        tz, tk = at_z(dz, dk)
        stage1.append(
            remote(tiles.at[tk], got.at[z, k], s1_send.at[n], s1_recv.at[n], device(x, y, tz, tk))
        )
    sibling = device(x, y, z, 1 - k)
    sib = [
        remote(val_hbm, val.at[k], sib_send.at[0], sib_recv.at[0], sibling),
        remote(scr_hbm, scr.at[k], sib_send.at[1], sib_recv.at[1], sibling),
    ]
    sent += stage1 + sib

    loads[1].wait()

    @pl.loop(0, 16)
    def _(t):
        r = pl.ds(pl.multiple_of(t * 64, 64), 64)
        for i in range(2):
            for xp in range(2):
                a = con[r, (4 * i + xp) * 128 : (4 * i + xp + 1) * 128]
                b = con[r, (4 * i + 2 + xp) * 128 : (4 * i + 3 + xp) * 128]
                low, high = halves(a, b)
                o = 512 * xp + 128 * i
                conp[r, o : o + 128] = low
                conp[r, o + 256 : o + 384] = high

    xcols = pl.ds(pl.multiple_of(x * 256, 256), 256)
    for copy in stage1:
        copy.wait_recv()
    for zh in range(2):
        for c in range(2):
            for i in range(2):
                low, high = halves(got[4 * zh + 2 * i, c], got[4 * zh + 2 * i + 1, c])
                cols = pl.ds(pl.multiple_of(x * 256 + i * 128, 128), 128)
                xall[zh, y, c, 0, :, cols] = low
                xall[zh, y, c, 1, :, cols] = high

    stage2 = []
    for n, d in enumerate(ring):
        own = xall.at[:, y, :, 0, :, xcols]
        stage2.append(remote(own, own, s2_send.at[0, n], s2_recv.at[0, n], ydev(d)))
        own = xall.at[:, y, :, 1, :, xcols]
        stage2.append(remote(own, own, s2_send.at[1, n], s2_recv.at[1, n], xdev(d)))
    sent += stage2

    loads[2].wait()
    sib[0].wait_recv()

    @pl.loop(0, 8)
    def _(t):
        p = t // 4
        r = pl.ds(pl.multiple_of((t % 4) * 256, 256), 256)
        val_t[:, pl.ds(pl.multiple_of(t * 256, 256), 256)] = val[p, r, :].T

    for copy in stage2:
        copy.wait_recv()
    stage3 = []
    for n, d in enumerate(ring):
        own = xall.at[:, :, :, 0, :, xcols]
        stage3.append(remote(own, own, s3_send.at[0, n], s3_recv.at[0, n], xdev(d)))
        own = xall.at[:, y, :, 1, :, :]
        stage3.append(remote(own, own, s3_send.at[1, n], s3_recv.at[1, n], ydev(d)))
    sent += stage3
    loads[3].wait()
    sib[1].wait_recv()
    for copy in stage3:
        copy.wait_recv()

    @pl.loop(0, 1024 // QT)
    def _(t):
        q = pl.ds(pl.multiple_of(t * QT, QT), QT)
        half[...] = dot_nt(xall[...].reshape(512, 1024), conp[q, :]).astype(BF16)
        for p in range(2):
            expanded = dot(val[p], half[...])
            weighted[p * 1024 : (p + 1) * 1024, :] = (
                expanded * scr[p, :, q].astype(F32)
            ).astype(BF16)
        back[:, q] = dot(val_t[...], weighted[...]).astype(BF16)

    recv1x, recv1y = [], []
    for j, d in enumerate(ring + (0,)):
        to = (x + d) % 4
        cols = pl.ds(pl.multiple_of(to * 256, 256), 256)
        block = dot(back[...], conp[:, cols]).reshape(2, 4, 2, 2, 16, 256)
        terms_f[:, :, :, :, :, cols] = block
        terms[:, :, :, :, :, cols] = block.astype(BF16)
        if d:
            recv1x.append(
                remote(terms.at[:, :, :, 0, :, cols], in_x.at[j], r1_send.at[j], r1_recv.at[j], xdev(d))
            )
        for n, dy in enumerate(ring):
            recv1y.append(
                remote(
                    terms.at[:, (y + dy) % 4, :, 1, :, cols], in_y.at[n, :, :, :, cols],
                    r1y_send.at[n, j], r1y_recv.at[n, j], ydev(dy),
                )
            )
    sent += recv1x + recv1y

    stage5 = []
    for copy in recv1x:
        copy.wait_recv()
    total = terms_f[:, :, :, 0, :, xcols]
    for n in range(3):
        total = total + in_x[n].astype(F32)
    sum1_f[...] = total
    sum1[...] = total.astype(BF16)
    for n, d in enumerate(ring):
        stage5.append(
            remote(sum1.at[:, (y + d) % 4], in2_y.at[n], r2_send.at[0, n], r2_recv.at[0, n], ydev(d))
        )
    for copy in recv1y:
        copy.wait_recv()
    total = terms_f[:, y, :, 1, :, :]
    for n in range(3):
        total = total + in_y[n].astype(F32)
    sum2_f[...] = total
    sum2[...] = total.astype(BF16)
    for n, d in enumerate(ring):
        cols = pl.ds(pl.multiple_of(((x + d) % 4) * 256, 256), 256)
        stage5.append(
            remote(sum2.at[:, :, :, cols], in2_x.at[n], r2_send.at[1, n], r2_recv.at[1, n], xdev(d))
        )
    sent += stage5
    for copy in stage5:
        copy.wait_recv()
    first = sum1_f[:, y]
    second = sum2_f[:, :, :, xcols]
    for n in range(3):
        first = first + in2_y[n].astype(F32)
        second = second + in2_x[n].astype(F32)
    for zh in range(2):
        for c in range(2):
            for i in range(2):
                cols = slice(128 * i, 128 * i + 128)
                pair = halves(first[zh, c, :, cols], second[zh, c, :, cols])
                for s in range(2):
                    pack_f[4 * zh + 2 * i + s, c] = pair[s]
                    pack[4 * zh + 2 * i + s, c] = pair[s].astype(BF16)

    stage6 = []
    for n, (dz, dk) in enumerate(zpeers):
        tz, tk = at_z(dz, dk)
        stage6.append(
            remote(pack.at[tz, tk], got3.at[n], r3_send.at[n], r3_recv.at[n], device(x, y, tz, tk))
        )
    sent += stage6
    for copy in stage6:
        copy.wait_recv()
    sums = [pack_f[z, k], None]
    for n, (dz, dk) in enumerate(zpeers):
        tile = got3[n].astype(F32)
        sums[dk] = tile if sums[dk] is None else sums[dk] + tile
    for dk in range(2):
        e = (k + dk) % 2
        tile = sums[dk].astype(BF16)
        out_ref[e, 0:16, :] = tile[:, :64]
        out_ref[e, 16:32, :] = tile[:, 64:]
    for copy in sent:
        copy.wait_send()


def local(excitons, screened, phi_val, phi_con):
    dma = pltpu.SemaphoreType.DMA
    vmem = pltpu.VMEM
    return pl.pallas_call(
        kernel,
        out_shape=jax.ShapeDtypeStruct((2, 32, 64), BF16),
        in_specs=[pl.BlockSpec(memory_space=pl.ANY)] * 4,
        out_specs=pl.BlockSpec(memory_space=pltpu.VMEM),
        scratch_shapes=[
            vmem((2, 32, 64), BF16),
            vmem((2, 16, 128), BF16),
            vmem((8, 2, 16, 128), BF16),
            vmem((1024, 1024), BF16),
            vmem((1024, 1024), BF16),
            vmem((2, 1024, 512), BF16),
            vmem((512, 2048), BF16),
            vmem((2, 1024, 1024), BF16),
            vmem((2, 4, 2, 2, 16, 1024), BF16),
            vmem((512, QT), BF16),
            vmem((2048, QT), BF16),
            vmem((512, 1024), BF16),
            vmem((2, 4, 2, 2, 16, 1024), F32),
            vmem((2, 4, 2, 2, 16, 1024), BF16),
            vmem((3, 2, 4, 2, 16, 256), BF16),
            vmem((3, 2, 2, 16, 1024), BF16),
            vmem((2, 4, 2, 16, 256), F32),
            vmem((2, 4, 2, 16, 256), BF16),
            vmem((2, 2, 16, 1024), F32),
            vmem((2, 2, 16, 1024), BF16),
            vmem((3, 2, 2, 16, 256), BF16),
            vmem((3, 2, 2, 16, 256), BF16),
            vmem((8, 2, 16, 128), F32),
            vmem((8, 2, 16, 128), BF16),
            vmem((15, 16, 128), BF16),
            dma((4,)),
            dma((2,)), dma((2,)),
            dma((15,)), dma((15,)),
            dma((2, 3)), dma((2, 3)),
            dma((2, 3)), dma((2, 3)),
            dma((3,)), dma((3,)),
            dma((3, 4)), dma((3, 4)),
            dma((2, 3)), dma((2, 3)),
            dma((15,)), dma((15,)),
        ],
        compiler_params=pltpu.CompilerParams(
            collective_id=0, has_side_effects=True, vmem_limit_bytes=56 * 2**20
        ),
        name="direct_kernel",
    )(excitons, screened, phi_val, phi_con)


def solution(mesh):
    placed = (P(None, "pa", "pb"), P("pa", "pb"), P("pa", None), P("pb", None))
    return jax.shard_map(
        local, mesh=mesh, in_specs=placed, out_specs=P(None, "pa", "pb"), check_vma=False
    )
```

time: 425 us -> 53.9 us (0.13)
  the two profiles are of different devices: /device:TPU:8 before, /device:TPU:1 now
where the time goes in v1:
time: 53.9 us; the launch traced here: 53.7 us
  Pallas kernels  52.3 us (97%)
  local copies, waits for them, and re-layouts  1.32 us (2%)
    pallas_call x1, Pallas kernels, local(): pl.pallas_call(kernel, out_shape=jax.ShapeDtypeStruct((2, 32, 64), BF16),...  52.3 us
    unnamed x1, local copies, waits for them, and re-layouts  1.32 us

profile of v1, /device:TPU:1, one launch (start us, length us, event | category | flops | bytes accessed | tf_op | source)
XLA Modules:
  0.0 53.7 jit_solution(8450100894875472547)
XLA Ops:
  0.0 52.3 %direct_kernel.1 = bf16[2,32,64]{2,1,0:T(8,128)(2,1)} custom-call(bf16[2,32,64]{2,1,0:T(8,128)(2,1)} %exc_hbm.1, bf16[1024,1024]{1,0:T(8,128)(2,1)} %scr_hbm.1, bf16[1024,512]{1,0:T(8,128)(2,1)} %val_hbm.1, bf16[1024,1024]{1,0:T(8,128)(2,1)} %con_hbm.1), custom_call_target="tpu_custom_call" | custom-call | tf_op jit(solution)/shard_map/direct_kernel/pallas_call | solution.py:258
  52.3 1.3 %copy.6 = bf16[2,32,64]{2,1,0:T(8,128)(2,1)} copy(bf16[2,32,64]{2,1,0:T(8,128)(2,1)} %direct_kernel.1) | data formatting | bytes 16384

commit v2 on v0

v2 whole, which is shorter than its diff:
```python
import jax
import jax.numpy as jnp
from jax import lax
from jax.experimental import pallas as pl
from jax.experimental.pallas import tpu as pltpu
from jax.sharding import PartitionSpec as P

F32, BF16 = jnp.float32, jnp.bfloat16
QT = 512
RING = (2, 1, 3)


def dot(a, b):
    return jnp.dot(a, b, preferred_element_type=F32)


def dot_nt(a, b):
    return lax.dot_general(a, b, (((1,), (1,)), ((), ())), preferred_element_type=F32)


def halves(a, b):
    low = jnp.concatenate([a[:, :64], b[:, :64]], axis=1)
    high = jnp.concatenate([a[:, 64:], b[:, 64:]], axis=1)
    return low, high


def kernel(
    exc_hbm, scr_hbm, val_hbm, con_hbm, out_ref,
    exc, tiles, got, con, conp, val, val_t, scr, xall, acc, half, weighted, back,
    terms_f, terms, in_x, in_y, sum1_f, sum1, sum2_f, sum2, in2_y, in2_x, pack_f, pack, got3,
    loc_sem, sib_send, sib_recv, s1_send, s1_recv, s2_send, s2_recv, s3_send, s3_recv,
    r1_send, r1_recv, r2_send, r2_recv, r3_send, r3_recv,
):
    pa, pb = lax.axis_index("pa"), lax.axis_index("pb")
    x, y, k = pb % 4, (pa // 2) % 4, pa % 2
    zh, i, s = pa // 8, pb // 8, (pb // 4) % 2

    def other(bit, d):
        return (bit + d) % 2

    def zdev(dzh, di, ds, dk):
        return (
            other(zh, dzh) * 8 + y * 2 + other(k, dk),
            (other(i, di) * 2 + other(s, ds)) * 4 + x,
        )

    def xdev(d):
        return (pa, pb - x + (x + d) % 4)

    def ydev(d):
        return (pa + (((y + d) % 4) - y) * 2, pb)

    def xcols(d=0):
        return pl.ds(pl.multiple_of(((x + d) % 4) * 128, 128), 128)

    far_first = [(1, 0), (1, 1), (0, 1), (0, 0)]
    zpeers = [
        (dzh, di, ds, dk) for dzh, di in far_first for ds in (1, 0) for dk in (0, 1)
        if (dzh, di, ds, dk) != (0, 0, 0, 0)
    ]

    barrier = pltpu.get_barrier_semaphore()

    def greet(who):
        pl.semaphore_signal(barrier, inc=1, device_id=who, device_id_type=pl.DeviceIdType.MESH)

    for peer in zpeers:
        greet(zdev(*peer))
    for d in RING:
        greet(xdev(d))
        greet(ydev(d))

    loads = [
        pltpu.make_async_copy(exc_hbm, exc, loc_sem.at[0]),
        pltpu.make_async_copy(con_hbm, con, loc_sem.at[1]),
        pltpu.make_async_copy(val_hbm, val.at[k], loc_sem.at[2]),
        pltpu.make_async_copy(scr_hbm, scr.at[k], loc_sem.at[3]),
    ]
    for load in loads:
        load.start()

    loads[0].wait()
    for e in range(2):
        tiles[e] = jnp.concatenate([exc[e, 0:16, :], exc[e, 16:32, :]], axis=1)
    got[zh, i, s, k] = tiles[k]

    pl.semaphore_wait(barrier, len(zpeers) + 2 * len(RING))

    def remote(src, dst, send, recv, who):
        copy = pltpu.make_async_remote_copy(
            src_ref=src, dst_ref=dst, send_sem=send, recv_sem=recv, device_id=who,
            device_id_type=pl.DeviceIdType.MESH,
        )
        copy.start()
        return copy

    stage1 = {}
    near = [p for p in zpeers if p[:2] == (0, 0)]
    for peer in near + [p for p in zpeers if p not in near]:
        dzh, di, ds, dk = peer
        stage1[peer] = remote(
            tiles.at[other(k, dk)], got.at[zh, i, s, k],
            s1_send.at[peer], s1_recv.at[peer], zdev(*peer),
        )
    sibling = zdev(0, 0, 0, 1)
    sib = [
        remote(val_hbm, val.at[k], sib_send.at[0], sib_recv.at[0], sibling),
        remote(scr_hbm, scr.at[k], sib_send.at[1], sib_recv.at[1], sibling),
    ]

    loads[1].wait()

    @pl.loop(0, 16)
    def _(t):
        r = pl.ds(pl.multiple_of(t * 64, 64), 64)
        for ii in range(2):
            for xp in range(2):
                a = con[r, (4 * ii + xp) * 128 : (4 * ii + xp + 1) * 128]
                b = con[r, (4 * ii + 2 + xp) * 128 : (4 * ii + 3 + xp) * 128]
                low, high = halves(a, b)
                o = 512 * ii + 256 * xp
                conp[r, o : o + 128] = low
                conp[r, o + 128 : o + 256] = high

    groups = [[(0, 0)], [(0, 1), (1, 1)], [(1, 0)]]

    def view(group):
        dzh, di = group[0]
        return (other(i, di), slice(None) if len(group) == 2 else pl.ds(other(zh, dzh), 1))

    stage2, stage3 = [], []
    for g, group in enumerate(groups):
        for dzh, di in group:
            for ds in range(2):
                for dk in range(2):
                    if (dzh, di, ds, dk) in stage1:
                        stage1[dzh, di, ds, dk].wait_recv()
        for dzh, di in group:
            tz, ti = other(zh, dzh), other(i, di)
            for c in range(2):
                low, high = halves(got[tz, ti, 0, c], got[tz, ti, 1, c])
                xall[ti, tz, y, c, 0, :, xcols()] = low
                xall[ti, tz, y, c, 1, :, xcols()] = high
        ti, tz = view(group)
        copies = []
        for n, d in enumerate(RING):
            own = xall.at[ti, tz, y, :, 0, :, xcols()]
            copies.append(remote(own, own, s2_send.at[g, 0, n], s2_recv.at[g, 0, n], ydev(d)))
            own = xall.at[ti, tz, y, :, 1, :, xcols()]
            copies.append(remote(own, own, s2_send.at[g, 1, n], s2_recv.at[g, 1, n], xdev(d)))
        stage2.append(copies)
    for g, group in enumerate(groups):
        for copy in stage2[g]:
            copy.wait_recv()
        ti, tz = view(group)
        copies = []
        for n, d in enumerate(RING):
            own = xall.at[ti, tz, :, :, 0, :, xcols()]
            copies.append(remote(own, own, s3_send.at[g, 0, n], s3_recv.at[g, 0, n], xdev(d)))
            own = xall.at[ti, tz, y, :, 1, :, :]
            copies.append(remote(own, own, s3_send.at[g, 1, n], s3_recv.at[g, 1, n], ydev(d)))
        stage3.append(copies)

    loads[2].wait()
    sib[0].wait_recv()

    @pl.loop(0, 8)
    def _(t):
        p = t // 4
        r = pl.ds(pl.multiple_of((t % 4) * 256, 256), 256)
        val_t[:, pl.ds(pl.multiple_of(t * 256, 256), 256)] = val[p, r, :].T

    def ccols(di):
        return pl.ds(pl.multiple_of(other(i, di) * 512, 512), 512)

    for g in (0, 1):
        for copy in stage3[g]:
            copy.wait_recv()

    @pl.loop(0, 1024 // QT)
    def _(t):
        q = pl.ds(pl.multiple_of(t * QT, QT), QT)
        rows = xall[other(i, 1)].reshape(512, 512)
        acc[:, :, q] = dot_nt(rows, conp[q, ccols(1)]).reshape(2, 256, QT)

    def finish(row):
        @pl.loop(0, 1024 // QT)
        def _(t):
            q = pl.ds(pl.multiple_of(t * QT, QT), QT)
            rows = xall[i, row].reshape(256, 512)
            half[row, :, q] = (acc[row, :, q] + dot_nt(rows, conp[q, ccols(0)])).astype(BF16)

    finish(zh)
    loads[3].wait()
    sib[1].wait_recv()
    for copy in stage3[2]:
        copy.wait_recv()
    finish(other(zh, 1))

    @pl.loop(0, 1024 // QT)
    def _(t):
        q = pl.ds(pl.multiple_of(t * QT, QT), QT)
        rows = half[:, :, q].reshape(512, QT)
        for p in range(2):
            expanded = dot(val[p], rows)
            weighted[p * 1024 : (p + 1) * 1024, q] = (
                expanded * scr[p, :, q].astype(F32)
            ).astype(BF16)

    scatter1 = []
    for g, (dzh, di) in enumerate(far_first):
        tz, ti = other(zh, dzh), other(i, di)
        if g % 2 == 0:
            r = pl.ds(pl.multiple_of(tz * 256, 256), 256)
            back[...] = dot(val_t[r, :], weighted[...]).astype(BF16)

        block = dot(back[...], conp[:, ccols(di)]).reshape(4, 2, 2, 16, 512)
        terms_f[g] = block
        terms[g] = block.astype(BF16)
        copies = [[], []]
        for n, d in enumerate(RING):
            copies[0].append(
                remote(terms.at[g, :, :, 0, :, xcols(d)], in_x.at[g, n], r1_send.at[g, 0, n], r1_recv.at[g, 0, n], xdev(d))
            )
            copies[1].append(
                remote(terms.at[g, (y + d) % 4, :, 1, :, :], in_y.at[g, n], r1_send.at[g, 1, n], r1_recv.at[g, 1, n], ydev(d))
            )
        scatter1.append(copies)

    scatter2, scatter3 = [], {}

    def reduce1(g):
        for copy in scatter1[g][0]:
            copy.wait_recv()
        total = terms_f[g, :, :, 0, :, xcols()]
        for n in range(3):
            total = total + in_x[g, n].astype(F32)
        sum1_f[g] = total
        sum1[g] = total.astype(BF16)
        copies = []
        for n, d in enumerate(RING):
            copies.append(
                remote(sum1.at[g, (y + d) % 4], in2_y.at[g, n], r2_send.at[g, 0, n], r2_recv.at[g, 0, n], ydev(d))
            )
        for copy in scatter1[g][1]:
            copy.wait_recv()
        total = terms_f[g, y, :, 1, :, :]
        for n in range(3):
            total = total + in_y[g, n].astype(F32)
        sum2_f[g] = total
        sum2[g] = total.astype(BF16)
        for n, d in enumerate(RING):
            copies.append(
                remote(sum2.at[g, :, :, xcols(d)], in2_x.at[g, n], r2_send.at[g, 1, n], r2_recv.at[g, 1, n], xdev(d))
            )
        scatter2.append(copies)

    def reduce2(g):
        for copy in scatter2[g]:
            copy.wait_recv()
        first = sum1_f[g, y]
        second = sum2_f[g, :, :, xcols()]
        for n in range(3):
            first = first + in2_y[g, n].astype(F32)
            second = second + in2_x[g, n].astype(F32)
        for c in range(2):
            for t, tile in enumerate(halves(first[c], second[c])):
                pack_f[g, t, c] = tile
                pack[g, t, c] = tile.astype(BF16)
        for ds in (1, 0):
            for dk in (0, 1):
                peer = (*far_first[g], ds, dk)
                if any(peer):
                    scatter3[peer] = remote(
                        pack.at[g, other(s, ds), other(k, dk)], got3.at[peer],
                        r3_send.at[peer], r3_recv.at[peer], zdev(*peer),
                    )

    for g in range(4):
        reduce1(g)
    for g in range(4):
        reduce2(g)

    sums = [pack_f[3, s, k], None]
    for peer, copy in scatter3.items():
        copy.wait_recv()
        tile = got3[peer].astype(F32)
        dk = peer[3]
        sums[dk] = tile if sums[dk] is None else sums[dk] + tile
    for dk in range(2):
        tile = sums[dk].astype(BF16)
        out_ref[other(k, dk), 0:16, :] = tile[:, :64]
        out_ref[other(k, dk), 16:32, :] = tile[:, 64:]

    for copy in list(stage1.values()) + sib + sum(stage2 + stage3, []):
        copy.wait_send()
    for copies in scatter1:
        for copy in copies[0] + copies[1]:
            copy.wait_send()
    for copy in sum(scatter2, []) + list(scatter3.values()):
        copy.wait_send()


def local(excitons, screened, phi_val, phi_con):
    dma = pltpu.SemaphoreType.DMA
    vmem = pltpu.VMEM
    return pl.pallas_call(
        kernel,
        out_shape=jax.ShapeDtypeStruct((2, 32, 64), BF16),
        in_specs=[pl.BlockSpec(memory_space=pl.ANY)] * 4,
        out_specs=pl.BlockSpec(memory_space=pltpu.VMEM),
        scratch_shapes=[
            vmem((2, 32, 64), BF16),
            vmem((2, 16, 128), BF16),
            vmem((2, 2, 2, 2, 16, 128), BF16),
            vmem((1024, 1024), BF16),
            vmem((1024, 1024), BF16),
            vmem((2, 1024, 512), BF16),
            vmem((512, 2048), BF16),
            vmem((2, 1024, 1024), BF16),
            vmem((2, 2, 4, 2, 2, 16, 512), BF16),
            vmem((2, 256, 1024), F32),
            vmem((2, 256, 1024), BF16),
            vmem((2048, 1024), BF16),
            vmem((256, 1024), BF16),
            vmem((4, 4, 2, 2, 16, 512), F32),
            vmem((4, 4, 2, 2, 16, 512), BF16),
            vmem((4, 3, 4, 2, 16, 128), BF16),
            vmem((4, 3, 2, 16, 512), BF16),
            vmem((4, 4, 2, 16, 128), F32),
            vmem((4, 4, 2, 16, 128), BF16),
            vmem((4, 2, 16, 512), F32),
            vmem((4, 2, 16, 512), BF16),
            vmem((4, 3, 2, 16, 128), BF16),
            vmem((4, 3, 2, 16, 128), BF16),
            vmem((4, 2, 2, 16, 128), F32),
            vmem((4, 2, 2, 16, 128), BF16),
            vmem((2, 2, 2, 2, 16, 128), BF16),
            dma((4,)),
            dma((2,)), dma((2,)),
            dma((2, 2, 2, 2)), dma((2, 2, 2, 2)),
            dma((3, 2, 3)), dma((3, 2, 3)),
            dma((3, 2, 3)), dma((3, 2, 3)),
            dma((4, 2, 3)), dma((4, 2, 3)),
            dma((4, 2, 3)), dma((4, 2, 3)),
            dma((2, 2, 2, 2)), dma((2, 2, 2, 2)),
        ],
        compiler_params=pltpu.CompilerParams(
            collective_id=0, has_side_effects=True, vmem_limit_bytes=56 * 2**20
        ),
        name="direct_kernel",
    )(excitons, screened, phi_val, phi_con)


def solution(mesh):
    placed = (P(None, "pa", "pb"), P("pa", "pb"), P("pa", None), P("pb", None))
    return jax.shard_map(
        local, mesh=mesh, in_specs=placed, out_specs=P(None, "pa", "pb"), check_vma=False
    )
```

time: 425 us -> 49.2 us (0.12)
  the two profiles are of different devices: /device:TPU:8 before, /device:TPU:1 now
where the time goes in v2:
time: 49.2 us; the launch traced here: 48.9 us
  Pallas kernels  47.6 us (97%)
  local copies, waits for them, and re-layouts  1.32 us (3%)
    pallas_call x1, Pallas kernels, local(): pl.pallas_call(kernel, out_shape=jax.ShapeDtypeStruct((2, 32, 64), BF16),...  47.6 us
    unnamed x1, local copies, waits for them, and re-layouts  1.32 us

profile of v2, /device:TPU:1, one launch (start us, length us, event | category | flops | bytes accessed | tf_op | source)
XLA Modules:
  0.0 48.9 jit_solution(564476247667775581)
XLA Ops:
  0.0 47.6 %direct_kernel.1 = bf16[2,32,64]{2,1,0:T(8,128)(2,1)} custom-call(bf16[2,32,64]{2,1,0:T(8,128)(2,1)} %exc_hbm.1, bf16[1024,1024]{1,0:T(8,128)(2,1)} %scr_hbm.1, bf16[1024,512]{1,0:T(8,128)(2,1)} %val_hbm.1, bf16[1024,1024]{1,0:T(8,128)(2,1)} %con_hbm.1), custom_call_target="tpu_custom_call" | custom-call | tf_op jit(solution)/shard_map/direct_kernel/pallas_call | solution.py:307
  47.6 1.3 %copy.6 = bf16[2,32,64]{2,1,0:T(8,128)(2,1)} copy(bf16[2,32,64]{2,1,0:T(8,128)(2,1)} %direct_kernel.1) | data formatting | bytes 16384

commit v3 on v2

--- a/solution.py
+++ b/solution.py
@@ -26,8 +26,8 @@
 
 def kernel(
     exc_hbm, scr_hbm, val_hbm, con_hbm, out_ref,
-    exc, tiles, got, con, conp, val, val_t, scr, xall, acc, half, weighted, back,
-    terms_f, terms, in_x, in_y, sum1_f, sum1, sum2_f, sum2, in2_y, in2_x, pack_f, pack, got3,
+    exc, tiles, got, con, conp, val, val_t, scr, first, second, xall, acc, half, weighted, back,
+    terms_f, terms, in1, sums1, in2, pack_f, pack, got3,
     loc_sem, sib_send, sib_recv, s1_send, s1_recv, s2_send, s2_recv, s3_send, s3_recv,
     r1_send, r1_recv, r2_send, r2_recv, r3_send, r3_recv,
 ):
@@ -52,6 +52,9 @@
 
     def xcols(d=0):
         return pl.ds(pl.multiple_of(((x + d) % 4) * 128, 128), 128)
+
+    def lanes(xx):
+        return pl.ds(pl.multiple_of(xx * 128, 128), 128)
 
     far_first = [(1, 0), (1, 1), (0, 1), (0, 0)]
     zpeers = [
@@ -122,44 +125,42 @@
                 conp[r, o : o + 128] = low
                 conp[r, o + 128 : o + 256] = high
 
-    groups = [[(0, 0)], [(0, 1), (1, 1)], [(1, 0)]]
-
-    def view(group):
-        dzh, di = group[0]
-        return (other(i, di), slice(None) if len(group) == 2 else pl.ds(other(zh, dzh), 1))
-
+    groups = [(0, 1), (1, 3), (3, 4)]
+    near_first = far_first[::-1]
     stage2, stage3 = [], []
-    for g, group in enumerate(groups):
-        for dzh, di in group:
+
+    def both(p, src, dst, send, recv, along):
+        start, stop = groups[p]
+        copies = []
+        for n, d in enumerate(RING):
+            for h, part, to in ((0, first, (ydev, xdev)[along](d)), (1, second, (xdev, ydev)[along](d))):
+                copies.append(
+                    remote(
+                        part.at[(slice(start, stop), *src)], part.at[(slice(start, stop), *dst(4 - d))],
+                        send.at[h, n], recv.at[h, n], to,
+                    )
+                )
+        return copies
+
+    for p, (start, stop) in enumerate(groups):
+        for g in range(start, stop):
+            dzh, di = near_first[g]
+            tz, ti = other(zh, dzh), other(i, di)
             for ds in range(2):
                 for dk in range(2):
                     if (dzh, di, ds, dk) in stage1:
                         stage1[dzh, di, ds, dk].wait_recv()
-        for dzh, di in group:
-            tz, ti = other(zh, dzh), other(i, di)
             for c in range(2):
                 low, high = halves(got[tz, ti, 0, c], got[tz, ti, 1, c])
-                xall[ti, tz, y, c, 0, :, xcols()] = low
-                xall[ti, tz, y, c, 1, :, xcols()] = high
-        ti, tz = view(group)
-        copies = []
-        for n, d in enumerate(RING):
-            own = xall.at[ti, tz, y, :, 0, :, xcols()]
-            copies.append(remote(own, own, s2_send.at[g, 0, n], s2_recv.at[g, 0, n], ydev(d)))
-            own = xall.at[ti, tz, y, :, 1, :, xcols()]
-            copies.append(remote(own, own, s2_send.at[g, 1, n], s2_recv.at[g, 1, n], xdev(d)))
-        stage2.append(copies)
-    for g, group in enumerate(groups):
-        for copy in stage2[g]:
+                first[g, 0, 0, c] = low
+                second[g, 0, 0, c] = high
+        stage2.append(both(p, (0, 0), lambda e: (0, e), s2_send.at[p], s2_recv.at[p], 0))
+        stage3.append(both(p, (0, 0), lambda e: (e, 0), s3_send.at[p, 0], s3_recv.at[p, 0], 1))
+    rest = slice(1, 4)
+    for p in range(3):
+        for copy in stage2[p]:
             copy.wait_recv()
-        ti, tz = view(group)
-        copies = []
-        for n, d in enumerate(RING):
-            own = xall.at[ti, tz, :, :, 0, :, xcols()]
-            copies.append(remote(own, own, s3_send.at[g, 0, n], s3_recv.at[g, 0, n], xdev(d)))
-            own = xall.at[ti, tz, y, :, 1, :, :]
-            copies.append(remote(own, own, s3_send.at[g, 1, n], s3_recv.at[g, 1, n], ydev(d)))
-        stage3.append(copies)
+        stage3[p] += both(p, (0, rest), lambda e: (e, rest), s3_send.at[p, 1], s3_recv.at[p, 1], 1)
 
     loads[2].wait()
     sib[0].wait_recv()
@@ -173,9 +174,19 @@
     def ccols(di):
         return pl.ds(pl.multiple_of(other(i, di) * 512, 512), 512)
 
-    for g in (0, 1):
-        for copy in stage3[g]:
+    def spread(p):
+        for copy in stage3[p]:
             copy.wait_recv()
+        for g in range(*groups[p]):
+            tz, ti = other(zh, near_first[g][0]), other(i, near_first[g][1])
+            for rx in range(4):
+                for ry in range(4):
+                    yy, xx = (y + ry) % 4, (x + rx) % 4
+                    xall[ti, tz, yy, :, 0, :, lanes(xx)] = first[g, rx, ry]
+                    xall[ti, tz, yy, :, 1, :, lanes(xx)] = second[g, ry, rx]
+
+    spread(0)
+    spread(1)
 
     @pl.loop(0, 1024 // QT)
     def _(t):
@@ -193,78 +204,70 @@
     finish(zh)
     loads[3].wait()
     sib[1].wait_recv()
-    for copy in stage3[2]:
-        copy.wait_recv()
+    for copy in list(stage1.values()) + sib + sum(stage2 + stage3, []):
+        copy.wait_send()
+    spread(2)
     finish(other(zh, 1))
 
-    @pl.loop(0, 1024 // QT)
-    def _(t):
-        q = pl.ds(pl.multiple_of(t * QT, QT), QT)
-        rows = half[:, :, q].reshape(512, QT)
-        for p in range(2):
-            expanded = dot(val[p], rows)
-            weighted[p * 1024 : (p + 1) * 1024, q] = (
-                expanded * scr[p, :, q].astype(F32)
-            ).astype(BF16)
-
-    scatter1 = []
-    for g, (dzh, di) in enumerate(far_first):
-        tz, ti = other(zh, dzh), other(i, di)
+    for p in range(2):
+        expanded = dot(val[p], half[...].reshape(512, 1024))
+        weighted[p * 1024 : (p + 1) * 1024, :] = (expanded * scr[p].astype(F32)).astype(BF16)
+
+    scatter1, scatter2, scatter3 = [], [], {}
+
+    def products(g):
+        dzh, di = far_first[g]
         if g % 2 == 0:
-            r = pl.ds(pl.multiple_of(tz * 256, 256), 256)
+            r = pl.ds(pl.multiple_of(other(zh, dzh) * 256, 256), 256)
             back[...] = dot(val_t[r, :], weighted[...]).astype(BF16)
-
-        block = dot(back[...], conp[:, ccols(di)]).reshape(4, 2, 2, 16, 512)
-        terms_f[g] = block
-        terms[g] = block.astype(BF16)
-        copies = [[], []]
-        for n, d in enumerate(RING):
-            copies[0].append(
-                remote(terms.at[g, :, :, 0, :, xcols(d)], in_x.at[g, n], r1_send.at[g, 0, n], r1_recv.at[g, 0, n], xdev(d))
+        block = dot(back[...], conp[:, ccols(di)])
+        for yy in range(4):
+            for xx in range(4):
+                cell = block[yy * 64 : yy * 64 + 64, xx * 128 : xx * 128 + 128].reshape(2, 2, 16, 128)
+                rx, ry = (xx + 4 - x) % 4, (yy + 4 - y) % 4
+                for h, to in enumerate(((rx, ry), (ry, rx))):
+                    terms_f[(h, g, *to)] = cell[:, h]
+                    terms[(h, g, *to)] = cell[:, h].astype(BF16)
+
+    def send1(g, m):
+        part = slice(0, 1) if m else slice(1, 4)
+        return [
+            remote(
+                terms.at[h, g, d, part], in1.at[h, g, n, part],
+                r1_send.at[g, m, h, n], r1_recv.at[g, m, h, n], (xdev, ydev)[h](d),
             )
-            copies[1].append(
-                remote(terms.at[g, (y + d) % 4, :, 1, :, :], in_y.at[g, n], r1_send.at[g, 1, n], r1_recv.at[g, 1, n], ydev(d))
-            )
-        scatter1.append(copies)
-
-    scatter2, scatter3 = [], {}
-
-    def reduce1(g):
+            for n, d in enumerate(RING) for h in range(2)
+        ]
+
+    def arrived1(h, g, m):
+        part = slice(0, 1) if m else slice(1, 4)
+        total = terms_f[h, g, 0, part]
+        for n in range(3):
+            total = total + in1[h, g, n, part].astype(F32)
+        return total
+
+    def send2(g):
         for copy in scatter1[g][0]:
             copy.wait_recv()
-        total = terms_f[g, :, :, 0, :, xcols()]
+        for h in range(2):
+            sums1[h, g] = arrived1(h, g, 0).astype(BF16)
+        scatter2.append([
+            remote(
+                sums1.at[h, g, d - 1], in2.at[h, g, n],
+                r2_send.at[g, h, n], r2_recv.at[g, h, n], (ydev, xdev)[h](d),
+            )
+            for n, d in enumerate(RING) for h in range(2)
+        ])
+        scatter1[g].append(send1(g, 1))
+
+    def send3(g):
+        for copy in scatter1[g][1] + scatter2[g]:
+            copy.wait_recv()
+        total = [arrived1(h, g, 1)[0] for h in range(2)]
         for n in range(3):
-            total = total + in_x[g, n].astype(F32)
-        sum1_f[g] = total
-        sum1[g] = total.astype(BF16)
-        copies = []
-        for n, d in enumerate(RING):
-            copies.append(
-                remote(sum1.at[g, (y + d) % 4], in2_y.at[g, n], r2_send.at[g, 0, n], r2_recv.at[g, 0, n], ydev(d))
-            )
-        for copy in scatter1[g][1]:
-            copy.wait_recv()
-        total = terms_f[g, y, :, 1, :, :]
-        for n in range(3):
-            total = total + in_y[g, n].astype(F32)
-        sum2_f[g] = total
-        sum2[g] = total.astype(BF16)
-        for n, d in enumerate(RING):
-            copies.append(
-                remote(sum2.at[g, :, :, xcols(d)], in2_x.at[g, n], r2_send.at[g, 1, n], r2_recv.at[g, 1, n], xdev(d))
-            )
-        scatter2.append(copies)
-
-    def reduce2(g):
-        for copy in scatter2[g]:
-            copy.wait_recv()
-        first = sum1_f[g, y]
-        second = sum2_f[g, :, :, xcols()]
-        for n in range(3):
-            first = first + in2_y[g, n].astype(F32)
-            second = second + in2_x[g, n].astype(F32)
+            total = [total[h] + in2[h, g, n].astype(F32) for h in range(2)]
         for c in range(2):
-            for t, tile in enumerate(halves(first[c], second[c])):
+            for t, tile in enumerate(halves(total[0][c], total[1][c])):
                 pack_f[g, t, c] = tile
                 pack[g, t, c] = tile.astype(BF16)
         for ds in (1, 0):
@@ -277,10 +280,15 @@
                     )
 
     for g in range(4):
-        reduce1(g)
+        products(g)
+        scatter1.append([send1(g, 0)])
     for g in range(4):
-        reduce2(g)
-
+        send2(g)
+    for g in range(4):
+        send3(g)
+
+    for copy in sum(scatter2 + sum(scatter1, []), []):
+        copy.wait_send()
     sums = [pack_f[3, s, k], None]
     for peer, copy in scatter3.items():
         copy.wait_recv()
@@ -292,12 +300,7 @@
         out_ref[other(k, dk), 0:16, :] = tile[:, :64]
         out_ref[other(k, dk), 16:32, :] = tile[:, 64:]
 
-    for copy in list(stage1.values()) + sib + sum(stage2 + stage3, []):
-        copy.wait_send()
-    for copies in scatter1:
-        for copy in copies[0] + copies[1]:
-            copy.wait_send()
-    for copy in sum(scatter2, []) + list(scatter3.values()):
+    for copy in scatter3.values():
         copy.wait_send()
 
 
@@ -318,21 +321,18 @@
             vmem((2, 1024, 512), BF16),
             vmem((512, 2048), BF16),
             vmem((2, 1024, 1024), BF16),
+            vmem((4, 4, 4, 2, 16, 128), BF16),
+            vmem((4, 4, 4, 2, 16, 128), BF16),
             vmem((2, 2, 4, 2, 2, 16, 512), BF16),
             vmem((2, 256, 1024), F32),
             vmem((2, 256, 1024), BF16),
             vmem((2048, 1024), BF16),
             vmem((256, 1024), BF16),
-            vmem((4, 4, 2, 2, 16, 512), F32),
-            vmem((4, 4, 2, 2, 16, 512), BF16),
-            vmem((4, 3, 4, 2, 16, 128), BF16),
-            vmem((4, 3, 2, 16, 512), BF16),
-            vmem((4, 4, 2, 16, 128), F32),
-            vmem((4, 4, 2, 16, 128), BF16),
-            vmem((4, 2, 16, 512), F32),
-            vmem((4, 2, 16, 512), BF16),
-            vmem((4, 3, 2, 16, 128), BF16),
-            vmem((4, 3, 2, 16, 128), BF16),
+            vmem((2, 4, 4, 4, 2, 16, 128), F32),
+            vmem((2, 4, 4, 4, 2, 16, 128), BF16),
+            vmem((2, 4, 3, 4, 2, 16, 128), BF16),
+            vmem((2, 4, 3, 2, 16, 128), BF16),
+            vmem((2, 4, 3, 2, 16, 128), BF16),
             vmem((4, 2, 2, 16, 128), F32),
             vmem((4, 2, 2, 16, 128), BF16),
             vmem((2, 2, 2, 2, 16, 128), BF16),
@@ -340,8 +340,8 @@
             dma((2,)), dma((2,)),
             dma((2, 2, 2, 2)), dma((2, 2, 2, 2)),
             dma((3, 2, 3)), dma((3, 2, 3)),
-            dma((3, 2, 3)), dma((3, 2, 3)),
-            dma((4, 2, 3)), dma((4, 2, 3)),
+            dma((3, 2, 2, 3)), dma((3, 2, 2, 3)),
+            dma((4, 2, 2, 3)), dma((4, 2, 2, 3)),
             dma((4, 2, 3)), dma((4, 2, 3)),
             dma((2, 2, 2, 2)), dma((2, 2, 2, 2)),
         ],

time: 49.2 us -> 48.4 us (0.984)
  Pallas kernels: 47.6 us -> 46.8 us
    pallas_call x1, Pallas kernels: 47.6 us -> 46.8 us  [local(): pl.pallas_call(kernel, out_shape=jax.ShapeDtypeStruct((2, 32, 64), BF16),...]
where the time goes in v3:
time: 48.4 us; the launch traced here: 48.1 us
  Pallas kernels  46.8 us (97%)
  local copies, waits for them, and re-layouts  1.32 us (3%)
    pallas_call x1, Pallas kernels, local(): pl.pallas_call(kernel, out_shape=jax.ShapeDtypeStruct((2, 32, 64), BF16),...  46.8 us
    unnamed x1, local copies, waits for them, and re-layouts  1.32 us

profile of v3, /device:TPU:1, one launch (start us, length us, event | category | flops | bytes accessed | tf_op | source)
XLA Modules:
  0.0 48.1 jit_solution(2467989831582573097)
XLA Ops:
  0.0 46.8 %direct_kernel.1 = bf16[2,32,64]{2,1,0:T(8,128)(2,1)} custom-call(bf16[2,32,64]{2,1,0:T(8,128)(2,1)} %exc_hbm.1, bf16[1024,1024]{1,0:T(8,128)(2,1)} %scr_hbm.1, bf16[1024,512]{1,0:T(8,128)(2,1)} %val_hbm.1, bf16[1024,1024]{1,0:T(8,128)(2,1)} %con_hbm.1), custom_call_target="tpu_custom_call" | custom-call | tf_op jit(solution)/shard_map/direct_kernel/pallas_call | solution.py:310
  46.8 1.3 %copy.6 = bf16[2,32,64]{2,1,0:T(8,128)(2,1)} copy(bf16[2,32,64]{2,1,0:T(8,128)(2,1)} %direct_kernel.1) | data formatting | bytes 16384

commit v4 on v3

--- a/solution.py
+++ b/solution.py
@@ -195,11 +195,8 @@
         acc[:, :, q] = dot_nt(rows, conp[q, ccols(1)]).reshape(2, 256, QT)
 
     def finish(row):
-        @pl.loop(0, 1024 // QT)
-        def _(t):
-            q = pl.ds(pl.multiple_of(t * QT, QT), QT)
-            rows = xall[i, row].reshape(256, 512)
-            half[row, :, q] = (acc[row, :, q] + dot_nt(rows, conp[q, ccols(0)])).astype(BF16)
+        rows = xall[i, row].reshape(256, 512)
+        half[row] = (acc[row] + dot_nt(rows, conp[:, ccols(0)])).astype(BF16)
 
     finish(zh)
     loads[3].wait()
@@ -247,17 +244,18 @@
         return total
 
     def send2(g):
-        for copy in scatter1[g][0]:
-            copy.wait_recv()
+        scatter2.append([])
         for h in range(2):
+            for copy in scatter1[g][0][h::2]:
+                copy.wait_recv()
             sums1[h, g] = arrived1(h, g, 0).astype(BF16)
-        scatter2.append([
-            remote(
-                sums1.at[h, g, d - 1], in2.at[h, g, n],
-                r2_send.at[g, h, n], r2_recv.at[g, h, n], (ydev, xdev)[h](d),
-            )
-            for n, d in enumerate(RING) for h in range(2)
-        ])
+            scatter2[g] += [
+                remote(
+                    sums1.at[h, g, d - 1], in2.at[h, g, n],
+                    r2_send.at[g, h, n], r2_recv.at[g, h, n], (ydev, xdev)[h](d),
+                )
+                for n, d in enumerate(RING)
+            ]
         scatter1[g].append(send1(g, 1))
 
     def send3(g):

time: 48.4 us -> 47.9 us (0.990)
  Pallas kernels: 46.8 us -> 46.3 us
    pallas_call x1, Pallas kernels: 46.8 us -> 46.3 us  [local(): pl.pallas_call(kernel, out_shape=jax.ShapeDtypeStruct((2, 32, 64), BF16),...]
where the time goes in v4:
time: 47.9 us; the launch traced here: 47.6 us
  Pallas kernels  46.3 us (97%)
  local copies, waits for them, and re-layouts  1.32 us (3%)
    pallas_call x1, Pallas kernels, local(): pl.pallas_call(kernel, out_shape=jax.ShapeDtypeStruct((2, 32, 64), BF16),...  46.3 us
    unnamed x1, local copies, waits for them, and re-layouts  1.32 us

profile of v4, /device:TPU:1, one launch (start us, length us, event | category | flops | bytes accessed | tf_op | source)
XLA Modules:
  0.0 47.6 jit_solution(9667867735933454003)
XLA Ops:
  0.0 46.3 %direct_kernel.1 = bf16[2,32,64]{2,1,0:T(8,128)(2,1)} custom-call(bf16[2,32,64]{2,1,0:T(8,128)(2,1)} %exc_hbm.1, bf16[1024,1024]{1,0:T(8,128)(2,1)} %scr_hbm.1, bf16[1024,512]{1,0:T(8,128)(2,1)} %val_hbm.1, bf16[1024,1024]{1,0:T(8,128)(2,1)} %con_hbm.1), custom_call_target="tpu_custom_call" | custom-call | tf_op jit(solution)/shard_map/direct_kernel/pallas_call | solution.py:308
  46.3 1.3 %copy.6 = bf16[2,32,64]{2,1,0:T(8,128)(2,1)} copy(bf16[2,32,64]{2,1,0:T(8,128)(2,1)} %direct_kernel.1) | data formatting | bytes 16384

commit v5 on v4

--- a/solution.py
+++ b/solution.py
@@ -6,7 +6,6 @@
 from jax.sharding import PartitionSpec as P
 
 F32, BF16 = jnp.float32, jnp.bfloat16
-QT = 512
 RING = (2, 1, 3)
 
 
@@ -188,11 +187,7 @@
     spread(0)
     spread(1)
 
-    @pl.loop(0, 1024 // QT)
-    def _(t):
-        q = pl.ds(pl.multiple_of(t * QT, QT), QT)
-        rows = xall[other(i, 1)].reshape(512, 512)
-        acc[:, :, q] = dot_nt(rows, conp[q, ccols(1)]).reshape(2, 256, QT)
+    acc[...] = dot_nt(xall[other(i, 1)].reshape(512, 512), conp[:, ccols(1)]).reshape(2, 256, 1024)
 
     def finish(row):
         rows = xall[i, row].reshape(256, 512)

time: 47.9 us -> 47.4 us (0.990)
  Pallas kernels: 46.3 us -> 45.8 us
where the time goes in v5:
time: 47.4 us; the launch traced here: 47.1 us
  Pallas kernels  45.8 us (97%)
  local copies, waits for them, and re-layouts  1.32 us (3%)
    pallas_call x1, Pallas kernels, local(): pl.pallas_call(kernel, out_shape=jax.ShapeDtypeStruct((2, 32, 64), BF16),...  45.8 us
    unnamed x1, local copies, waits for them, and re-layouts  1.32 us

profile of v5, /device:TPU:1, one launch (start us, length us, event | category | flops | bytes accessed | tf_op | source)
XLA Modules:
  0.0 47.1 jit_solution(13217611626742001548)
XLA Ops:
  0.0 45.8 %direct_kernel.1 = bf16[2,32,64]{2,1,0:T(8,128)(2,1)} custom-call(bf16[2,32,64]{2,1,0:T(8,128)(2,1)} %exc_hbm.1, bf16[1024,1024]{1,0:T(8,128)(2,1)} %scr_hbm.1, bf16[1024,512]{1,0:T(8,128)(2,1)} %val_hbm.1, bf16[1024,1024]{1,0:T(8,128)(2,1)} %con_hbm.1), custom_call_target="tpu_custom_call" | custom-call | tf_op jit(solution)/shard_map/direct_kernel/pallas_call | solution.py:303
  45.8 1.3 %copy.6 = bf16[2,32,64]{2,1,0:T(8,128)(2,1)} copy(bf16[2,32,64]{2,1,0:T(8,128)(2,1)} %direct_kernel.1) | data formatting | bytes 16384
